TPU v7x, 32 devices: a whole 2x2x4 slice. The times are simulated.
32 devices in a mesh: group: 2 (over y), wide: 4 (over z), narrow: 2 (over x), deep: 2 (over core).
Axes of the slice: x: 2, y: 2, z: 4, core: 2. Of those that a mesh axis runs over, the one named last changes fastest.
Arguments:
- queries: bfloat16 [384, 4096], P(('group', 'wide', 'deep'), 'narrow'), parts along dimension 0, may hold values from -110 to 110
- cache_keys: bfloat16 [384, 4, 32, 128], P(('group', 'wide', 'deep'), 'narrow'), parts along dimension 0, may hold values from -4.1 to 4.1
- cache_values: bfloat16 [384, 4, 32, 128], P(('group', 'wide', 'deep'), 'narrow'), parts along dimension 0, may hold values from -6 to 6
- fresh_pairs: bfloat16 [384, 2, 512], P(('group', 'wide', 'deep'), None, 'narrow'), parts along dimension 0, may hold values from -6 to 6
- lengths: int32 [384], P(('group', 'wide', 'deep')), parts along dimension 0, may hold values from 2 to 32, as said below
- residual: bfloat16 [384, 2048], P(('group', 'wide', 'deep')), parts along dimension 0, may hold values from -6 to 6
- norm_gain: float32 [2048], replicated, may hold values from 0.1 to 1.9
- output_weight: bfloat16 [4096, 2048], P('narrow', 'deep'), may hold values from -0.09375 to 0.09375
- expert_gate_up: bfloat16 [8, 2, 768, 2048], P(('wide', 'deep'), None, 'narrow'), may hold values from -0.125 to 0.125
- expert_down: bfloat16 [8, 768, 2048], P(('wide', 'deep'), None, 'narrow'), may hold values from -0.21875 to 0.21875
- routed_experts: int32 [384, 1], P(('group', 'wide', 'deep')), parts along dimension 0, may hold values from 0 to 7, as said below
- router_weights: float32 [384, 1], P(('group', 'wide', 'deep')), parts along dimension 0, may hold values from 0.1 to 1
Outputs:
- layer_out: bfloat16 [384, 2048], P(('group', 'wide', 'deep'), 'narrow'), parts along dimension 0
There are 2 independent parts, one for each index of `group`. A program takes and returns all parts, laid end to end along the dimension named above; an argument that names none is the same for every part. Nothing has to cross between parts.
Inputs may be any that keep to these rules, and one draw needn't show every extreme that they name: `routed_experts`: each row names 1 different experts. Among the rows of one device no expert is named more than 6 times, and one and the same expert is named exactly 6 times by the rows of every device. `lengths`: each device's block of 24 requests holds one of length 32.
All inputs are finite; a program needn't handle non-finite values.
Results may differ from a plain program's by a relative error of at most 0.0095.
Values may be sent and summed in bfloat16 or wider, within the bound.
A program may use at most 64 MiB of HBM per device.

v0:
```python
import math

import jax
import jax.numpy as jnp
from jax import lax
from jax.sharding import PartitionSpec as P


def shards(
    queries,
    cache_keys,
    cache_values,
    fresh_pairs,
    lengths,
    residual,
    norm_gain,
    output_weight,
    expert_gate_up,
    expert_down,
    routed_experts,
    router_weights,
):
    row_count = queries.shape[0]
    local_heads = cache_keys.shape[1]
    length = cache_keys.shape[2]
    head_size = cache_keys.shape[3]
    group_size = queries.shape[1] // (local_heads * head_size)
    score_scale = 1.0 / math.sqrt(head_size)
    query_heads = queries.reshape(row_count, local_heads, group_size, head_size)
    fresh_heads = fresh_pairs.reshape(row_count, 2, local_heads, head_size)
    scores = (
        jnp.einsum("rkgd,rkld->rkgl", query_heads, cache_keys, preferred_element_type=jnp.float32)
        * score_scale
    )
    in_cache = jnp.arange(length, dtype=jnp.int32)[None, :] < lengths[:, None]
    scores = jnp.where(in_cache[:, None, None, :], scores, -1e30)
    own_score = (
        jnp.einsum(
            "rkgd,rkd->rkg", query_heads, fresh_heads[:, 0], preferred_element_type=jnp.float32
        )
        * score_scale
    )
    row_max = jnp.maximum(jnp.max(scores, -1), own_score)
    weights_raw = jnp.exp(scores - row_max[..., None])
    own_raw = jnp.exp(own_score - row_max)
    denominator = jnp.sum(weights_raw, -1) + own_raw
    attention_weights = (weights_raw / denominator[..., None]).astype(jnp.bfloat16)
    own_weight = (own_raw / denominator).astype(jnp.bfloat16)
    attended = jnp.einsum(
        "rkgl,rkld->rkgd", attention_weights, cache_values, preferred_element_type=jnp.float32
    )
    attended = (
        attended
        + own_weight.astype(jnp.float32)[..., None]
        * fresh_heads[:, 1].astype(jnp.float32)[:, :, None, :]
    )
    attended = attended.astype(jnp.bfloat16).reshape(row_count, -1)
    paired = jnp.dot(
        lax.all_gather(attended, "deep", axis=0, tiled=True),
        output_weight,
        preferred_element_type=jnp.float32,
    )
    partial_value = lax.all_to_all(
        paired.astype(jnp.bfloat16), "deep", split_axis=0, concat_axis=1, tiled=True
    ).astype(paired.dtype)
    full_width = residual.shape[1]
    narrow_count = lax.axis_size("narrow")
    narrow_index = lax.axis_index("narrow")
    share_width = full_width // narrow_count
    experts = lax.axis_size(("wide", "deep"))
    picks_per_row = routed_experts.shape[1]
    capacity = row_count // 4
    pick_count = row_count * picks_per_row
    weights = router_weights / jnp.sum(router_weights, -1, keepdims=True)
    flat_experts = routed_experts.reshape(-1)
    expert_hits = (flat_experts[:, None] == jnp.arange(experts, dtype=jnp.int32)[None, :]).astype(
        jnp.int32
    )
    slot_index = jnp.sum((jnp.cumsum(expert_hits, 0) - expert_hits) * expert_hits, 1)
    target = flat_experts * capacity + slot_index
    placing = (jnp.arange(experts * capacity, dtype=jnp.int32)[:, None] == target[None, :]).astype(
        jnp.bfloat16
    )
    owner_map = (
        jnp.arange(pick_count, dtype=jnp.int32)[:, None] // picks_per_row
        == jnp.arange(row_count, dtype=jnp.int32)[None, :]
    ).astype(jnp.bfloat16)
    spread = jnp.dot(placing, owner_map, preferred_element_type=jnp.float32).astype(jnp.bfloat16)
    gate_up = expert_gate_up[0]
    down_local = expert_down[0]
    share = lax.psum_scatter(
        partial_value.astype(jnp.bfloat16), "narrow", scatter_dimension=1, tiled=True
    ).astype(jnp.float32)
    mixed_mine = (
        lax.dynamic_slice_in_dim(residual, narrow_index * share_width, share_width, 1).astype(
            jnp.float32
        )
        + share
    )
    squares = lax.psum(jnp.sum(mixed_mine * mixed_mine, -1, keepdims=True), "narrow")
    gain_mine = lax.dynamic_slice_in_dim(norm_gain, narrow_index * share_width, share_width, 0)
    normed = (mixed_mine * lax.rsqrt(squares / full_width + 1e-06) * gain_mine).astype(jnp.bfloat16)
    outgoing = (
        jnp.dot(spread, normed, preferred_element_type=jnp.float32)
        .astype(jnp.bfloat16)
        .reshape(experts, capacity, share_width)
    )
    incoming = lax.all_to_all(
        outgoing, ("wide", "deep"), split_axis=0, concat_axis=0, tiled=True
    ).reshape(experts * capacity, share_width)
    both_parts = jnp.einsum(
        "nd,gfd->gnf",
        lax.all_gather(incoming, "narrow", axis=1, tiled=True),
        gate_up,
        preferred_element_type=jnp.float32,
    )
    hidden_act = (jax.nn.silu(both_parts[0]) * both_parts[1]).astype(jnp.bfloat16)
    expert_share = jnp.dot(
        lax.all_gather(hidden_act, "narrow", axis=1, tiled=True),
        down_local,
        preferred_element_type=jnp.float32,
    ).astype(jnp.bfloat16)
    returned = lax.all_to_all(
        expert_share.reshape(experts, capacity, share_width),
        ("wide", "deep"),
        split_axis=0,
        concat_axis=0,
        tiled=True,
    )
    chosen = jnp.take(returned.reshape(experts * capacity, share_width), target, axis=0)
    chosen = chosen.reshape(row_count, picks_per_row, share_width).astype(jnp.float32)
    combined = jnp.sum(chosen * weights[:, :, None], 1)
    return (mixed_mine + combined).astype(jnp.bfloat16)


def solution(mesh):
    in_specs = (
        P(("group", "wide", "deep"), "narrow"),
        P(("group", "wide", "deep"), "narrow", None, None),
        P(("group", "wide", "deep"), "narrow", None, None),
        P(("group", "wide", "deep"), None, "narrow"),
        P(("group", "wide", "deep")),
        P(("group", "wide", "deep"), None),
        P(),
        P("narrow", "deep"),
        P(("wide", "deep"), None, "narrow", None),
        P(("wide", "deep"), None, "narrow"),
        P(("group", "wide", "deep"), None),
        P(("group", "wide", "deep"), None),
    )
    out_specs = P(("group", "wide", "deep"), "narrow")
    return jax.shard_map(shards, mesh=mesh, in_specs=in_specs, out_specs=out_specs, check_vma=False)
```

profile of v0, /device:TPU:0, one launch (start us, length us, event | category | flops | bytes accessed | tf_op | source)
XLA Modules:
  0.0 82.3 jit_solution(6561578115436360470)
XLA Ops:
  6.5 0.0 copy-start
  6.5 0.0 reduce-scatter.2.cloned.1.call-start
  6.5 1.1 %copy.21 = bf16[3,8,16,128]{3,2,1,0:T(8,128)(2,1)S(1)} copy(bf16[3,8,16,128]{3,1,2,0:T(8,128)(2,1)} %bitcast.77) | data formatting | bytes 196608
  7.6 0.7 iota_compare_fusion.5
  8.3 0.8 reshape.108
  9.1 0.0 copy-start.1
  9.1 0.2 fusion.21
  9.3 1.6 %fusion.30 = (f32[24,2,8]{2,1,0:T(2,128)S(1)}, f32[24,2,8,32]{3,2,1,0:T(8,128)S(1)}) fusion(bf16[24,2,8,128]{3,2,1,0:T(8,128)(2,1)S(1)} %bitcast.75, bf16[24,2,32,128]{3,2,1,0:T(8,128)(2,1)} %param.13, pred[24,32]{1,0:T(8,128)(4,1)S(1)} %iota_compare_fusion.5), kind=kOutput, calls=%fused_computation.57 | convolution fusion | flops 3182208 | bytes 542976 | tf_op jit(solution)/shard_map/rkgd,rkld->rkgl/dot_general | solution.py:32
  10.9 0.2 fusion.13
  11.2 1.3 %fusion.5 = bf16[24,2,8,128]{3,2,1,0:T(8,128)(2,1)S(1)} fusion(bf16[24,2,32,128]{3,2,1,0:T(8,128)(2,1)} %param.14, f32[24,2,8,32]{3,2,1,0:T(8,128)S(1)} %get-tuple-element.12, f32[24,2,128]{2,1,0:T(2,128)S(1)} %get-tuple-element.10, f32[24,2,8]{2,1,0:T(2,128)S(1)} %get-tuple-element.8, f32[24,2,8]{2,1,0:T(2,128)S(1)} %get-tuple-element.7, ...), kind=kOutput, calls=%fused_computation.8 | convolution fusion | flops 3330048 | bytes 569856 | tf_op jit(solution)/shard_map/rkgl,rkld->rkgd/dot_general | solution.py:49
  12.5 0.0 copy-start.5
  12.5 0.0 copy-start.6
  12.5 0.0 copy-start.4
  12.6 2.0 %all_gather.9 = bf16[48,2048]{1,0:T(8,128)(2,1)S(1)} all-gather(bf16[24,2048]{1,0:T(8,128)(2,1)S(1)} %bitcast.73), channel_id=1, replica_groups=mesh['group'=2,'wide'=4,'narrow'=2,'deep'=2] {'deep'}, dimensions={0}, use_global_device_ids=true | all-gather | bytes 294912 | tf_op jit(solution)/shard_map/all_gather | solution.py:59
  14.6 0.0 copy-done.1
  14.6 0.8 %convolution_convert_fusion.1 = bf16[48,1024]{1,0:T(8,128)(2,1)S(1)} fusion(bf16[48,2048]{1,0:T(8,128)(2,1)S(1)} %all_gather.9, bf16[2048,1024]{1,0:T(8,128)(2,1)S(1)} %copy-done.1), kind=kOutput, calls=%fused_computation.12 | convolution fusion | flops 201375744 | bytes 4489216 | tf_op jit(solution)/shard_map/dot_general | solution.py:58
  15.5 3.8 %all_to_all.29 = bf16[2,24,1024]{2,1,0:T(8,128)(2,1)S(1)} all-to-all(bf16[2,24,1024]{2,1,0:T(8,128)(2,1)S(1)} %bitcast.76), channel_id=1, replica_groups=mesh['group'=2,'wide'=4,'narrow'=2,'deep'=2] {'deep'}, dimensions={0} | all-to-all | bytes 196608 | tf_op jit(solution)/shard_map/all_to_all | solution.py:63
  19.3 0.6 copy.20
  19.9 0.0 reduce-scatter.2.cloned.1.call-update
  19.9 0.0 copy-done.5
  19.9 0.1 fusion.26
  20.1 0.2 select_reduce_fusion
  20.2 0.0 copy-done.6
  20.3 12.4 %reduce-scatter.2.cloned.1.call-done = bf16[24,1024]{1,0:T(8,128)(2,1)} async-done(((bf16[24,2048]{1,0:T(8,128)(2,1)}), bf16[24,1024]{1,0:T(8,128)(2,1)}) %reduce-scatter.2.cloned.1.call-update) | async-done | bytes 49168 | tf_op jit(solution)/shard_map/reduce_scatter | solution.py:91
  32.6 0.0 copy-done.4
  32.6 0.9 %multiply_reduce_fusion = f32[24]{0:T(128)S(1)} fusion(bf16[24,1024]{1,0:T(8,128)(2,1)} %reduce-scatter.2.cloned.1.call-done, bf16[24,2048]{1,0:T(8,128)(2,1)S(1)} %copy-done.4, s32[]{:T(128)S(6)} %select_n.26), kind=kLoop, calls=%fused_computation.21 | loop fusion | flops 122856 | bytes 98404 | tf_op jit(solution)/shard_map/reduce_sum | solution.py:100
  33.6 4.9 %psum.7 = f32[24,1]{0,1:T(1,128)S(1)} all-reduce(f32[24,1]{0,1:T(1,128)S(1)} %bitcast.84), channel_id=1, replica_groups=mesh['group'=2,'wide'=4,'narrow'=2,'deep'=2] {'narrow'}, use_global_device_ids=true, to_apply=%region_6.7 | all-reduce | flops 24 | bytes 192 | tf_op jit(solution)/shard_map/psum | solution.py:100
  38.5 1.1 %convolution_convert_fusion = bf16[48,1024]{1,0:T(8,128)(2,1)S(1)} fusion(bf16[24,1024]{1,0:T(8,128)(2,1)} %reduce-scatter.2.cloned.1.call-done, f32[1024]{0:T(1024)S(1)} %dynamic_slice.7, f32[24]{0:T(128)S(1)} %rsqrt_bitcast_fusion, bf16[24,2048]{1,0:T(8,128)(2,1)S(1)} %copy-done.4, s32[]{:T(128)S(6)} %select_n.26, s32[24]{0:T(128)S(1)} %multiply_add_fusion), kind=kOutput, calls=%fused_computation.11 | convolution fusion | flops 2614080 | bytes 201732 | tf_op jit(solution)/shard_map/dot_general | solution.py:104
  39.6 0.7 reshape.110
  40.3 4.6 %all-to-all-start.1 = ((bf16[8,6,1024]{2,1,0:T(8,128)(2,1)}), bf16[8,6,1024]{2,1,0:T(8,128)(2,1)S(1)}, u32[]{:S(2)}, u32[]{:S(2)}) async-start(bf16[8,6,1024]{2,1,0:T(8,128)(2,1)} %reshape.110), calls=%async_computation.2 | async-start | bytes 262144 | tf_op jit(solution)/shard_map/all_to_all | solution.py:108
  44.9 6.8 %all-to-all-done.1 = bf16[8,6,1024]{2,1,0:T(8,128)(2,1)S(1)} async-done(((bf16[8,6,1024]{2,1,0:T(8,128)(2,1)}), bf16[8,6,1024]{2,1,0:T(8,128)(2,1)S(1)}, u32[]{:S(2)}, u32[]{:S(2)}) %all-to-all-start.1) | async-done | bytes 98336 | tf_op jit(solution)/shard_map/all_to_all | solution.py:108
  51.7 0.0 copy-start.2
  51.7 0.0 copy-start.7
  51.7 5.4 %all_gather.10 = bf16[48,2048]{1,0:T(8,128)(2,1)S(1)} all-gather(bf16[48,1024]{1,0:T(8,128)(2,1)S(1)} %reshape.111), channel_id=1, replica_groups=mesh['group'=2,'wide'=4,'narrow'=2,'deep'=2] {'narrow'}, dimensions={1}, use_global_device_ids=true | all-gather | bytes 294912 | tf_op jit(solution)/shard_map/all_gather | solution.py:113
  57.1 0.0 copy-done
  57.2 0.0 copy-start.3
  57.2 1.1 %fusion.9 = f32[2,48,384]{2,1,0:T(8,128)S(1)} fusion(bf16[1,2,384,2048]{3,2,1,0:T(8,128)(2,1)S(1)} %copy-done, bf16[48,2048]{1,0:T(8,128)(2,1)S(1)} %all_gather.10), kind=kOutput, calls=%fused_computation.10 | convolution fusion | flops 150994944 | bytes 3489792 | tf_op jit(solution)/shard_map/nd,gfd->gnf/dot_general | solution.py:111
  58.3 4.6 %all_gather.11 = bf16[48,768]{1,0:T(8,128)(2,1)S(1)} all-gather(bf16[48,384]{1,0:T(8,128)(2,1)S(1)} %fusion.17), channel_id=1, replica_groups=mesh['group'=2,'wide'=4,'narrow'=2,'deep'=2] {'narrow'}, dimensions={1}, use_global_device_ids=true | all-gather | bytes 110592 | tf_op jit(solution)/shard_map/all_gather | solution.py:119
  62.9 0.0 copy-done.2
  62.9 0.4 fusion.6
  63.3 0.7 reshape.112
  64.0 3.4 %all-to-all-start.2 = ((bf16[8,6,1024]{2,1,0:T(8,128)(2,1)}), bf16[8,6,1024]{2,1,0:T(8,128)(2,1)S(1)}, u32[]{:S(2)}, u32[]{:S(2)}) async-start(bf16[8,6,1024]{2,1,0:T(8,128)(2,1)} %reshape.112), calls=%async_computation.3 | async-start | bytes 262144 | tf_op jit(solution)/shard_map/all_to_all | solution.py:123
  67.3 0.0 copy-done.7
  67.4 6.7 %all-to-all-done.2 = bf16[8,6,1024]{2,1,0:T(8,128)(2,1)S(1)} async-done(((bf16[8,6,1024]{2,1,0:T(8,128)(2,1)}), bf16[8,6,1024]{2,1,0:T(8,128)(2,1)S(1)}, u32[]{:S(2)}, u32[]{:S(2)}) %all-to-all-start.2) | async-done | bytes 98336 | tf_op jit(solution)/shard_map/all_to_all | solution.py:123
  74.1 0.6 gather_fusion
  74.7 0.0 copy-done.3
  74.7 0.7 add_convert_fusion
  (14 shorter events, 0.3 us)
Async XLA Ops:
  6.5 50.6 %copy-start = (bf16[1,2,384,2048]{3,2,1,0:T(8,128)(2,1)S(1)}, bf16[1,2,384,2048]{3,2,1,0:T(8,128)(2,1)}, u32[]{:S(2)}) copy-start(bf16[1,2,384,2048]{3,2,1,0:T(8,128)(2,1)} %param.20) | copy-start | bytes 9437188
  6.5 26.1 %reduce-scatter.2.cloned.1.call-start = ((), (), s32[]{:S(2)}) async-start(), calls=%async_computation.4 | async-start | bytes 147456 | tf_op jit(solution)/shard_map/reduce_scatter | solution.py:91
  9.1 5.5 %copy-start.1 = (bf16[2048,1024]{1,0:T(8,128)(2,1)S(1)}, bf16[2048,1024]{1,0:T(8,128)(2,1)}, u32[]{:S(2)}) copy-start(bf16[2048,1024]{1,0:T(8,128)(2,1)} %param.19) | copy-start | bytes 12582916
  12.5 7.4 %copy-start.5 = (s32[24,1]{0,1:T(1,128)S(1)}, s32[24,1]{0,1:T(1,128)}, u32[]{:S(2)}) copy-start(s32[24,1]{0,1:T(1,128)} %param.22) | copy-start | bytes 292
  12.5 7.7 %copy-start.6 = (f32[2048]{0:T(1024)S(1)}, f32[2048]{0:T(1024)}, u32[]{:S(2)}) copy-start(f32[2048]{0:T(1024)} %param.18) | copy-start | bytes 24580
  12.5 20.1 %copy-start.4 = (bf16[24,2048]{1,0:T(8,128)(2,1)S(1)}, bf16[24,2048]{1,0:T(8,128)(2,1)}, u32[]{:S(2)}) copy-start(bf16[24,2048]{1,0:T(8,128)(2,1)} %param.17) | copy-start | bytes 294916
  40.3 11.4 %all-to-all-start.1 = ((bf16[8,6,1024]{2,1,0:T(8,128)(2,1)}), bf16[8,6,1024]{2,1,0:T(8,128)(2,1)S(1)}, u32[]{:S(2)}, u32[]{:S(2)}) async-start(bf16[8,6,1024]{2,1,0:T(8,128)(2,1)} %reshape.110), calls=%async_computation.2 | async-start | bytes 262144 | tf_op jit(solution)/shard_map/all_to_all | solution.py:108
  51.7 11.2 %copy-start.2 = (bf16[1,768,1024]{2,1,0:T(8,128)(2,1)S(1)}, bf16[1,768,1024]{2,1,0:T(8,128)(2,1)}, u32[]{:S(2)}) copy-start(bf16[1,768,1024]{2,1,0:T(8,128)(2,1)} %param.21) | copy-start | bytes 4718596
  51.7 15.6 %copy-start.7 = (f32[24,1]{0,1:T(1,128)S(1)}, f32[24,1]{0,1:T(1,128)}, u32[]{:S(2)}) copy-start(f32[24,1]{0,1:T(1,128)} %param.23) | copy-start | bytes 292
  57.2 17.6 %copy-start.3 = (bf16[24,1024]{1,0:T(8,128)(2,1)S(1)}, bf16[24,1024]{1,0:T(8,128)(2,1)}, u32[]{:S(2)}) copy-start(bf16[24,1024]{1,0:T(8,128)(2,1)} %reduce-scatter.2.cloned.1.call-done) | copy-start | bytes 147460
  64.0 10.1 %all-to-all-start.2 = ((bf16[8,6,1024]{2,1,0:T(8,128)(2,1)}), bf16[8,6,1024]{2,1,0:T(8,128)(2,1)S(1)}, u32[]{:S(2)}, u32[]{:S(2)}) async-start(bf16[8,6,1024]{2,1,0:T(8,128)(2,1)} %reshape.112), calls=%async_computation.3 | async-start | bytes 262144 | tf_op jit(solution)/shard_map/all_to_all | solution.py:123
Sparse Core Ops, SparseCore 0:
  20.0 12.5 reduce-scatter.1
where the time goes:
time: 82.8 us; the launch traced here: 82.3 us
  waiting for transfers between devices  25.8 us (31%)
  blocking collectives  20.8 us (25%)
  between operations  13.6 us (16%)
  starting transfers between devices  7.98 us (10%)
  matrix products  6.37 us (8%)
  local copies, waits for them, and re-layouts  4.57 us (6%)
  other arithmetic  3.07 us (4%)
    reduce_scatter x1, waiting for transfers between devices, shards(): lax.psum_scatter(partial_value.astype(jnp.bfloat16), 'narrow', scatter_di...  12.4 us
    all_to_all x1, waiting for transfers between devices, shards(): lax.all_to_all(outgoing, ('wide', 'deep'), split_axis=0, concat_axis=0, t...  6.76 us
    all_to_all x1, waiting for transfers between devices, shards(): lax.all_to_all(expert_share.reshape(experts, capacity, share_width), ('wi...  6.69 us
    all_gather x1, blocking collectives, shards(): lax.all_gather(incoming, 'narrow', axis=1, tiled=True)  5.43 us
    psum x1, blocking collectives, shards(): lax.psum(jnp.sum(mixed_mine * mixed_mine, -1, keepdims=True), 'narrow')  4.94 us
    all_gather x1, blocking collectives, shards(): lax.all_gather(hidden_act, 'narrow', axis=1, tiled=True)  4.64 us
    all_to_all x1, starting transfers between devices, shards(): lax.all_to_all(outgoing, ('wide', 'deep'), split_axis=0, concat_axis=0, t...  4.61 us
    all_to_all x1, blocking collectives, shards(): lax.all_to_all(paired.astype(jnp.bfloat16), 'deep', split_axis=0, concat_...  3.79 us
  transfers between devices with their start and end apart: 3, of which 3 were waited for; matrix products, arithmetic and copies ran while one was open for 0% of the time, Pallas kernels for 0%

commit v1 on v0

v1 whole, which is shorter than its diff:
```python
import functools
import math

import jax
import jax.numpy as jnp
from jax import lax
from jax.experimental import pallas as pl
from jax.experimental.pallas import tpu as pltpu
from jax.sharding import PartitionSpec as P

BF = jnp.bfloat16
F32 = jnp.float32
MESH = pl.DeviceIdType.MESH


def up_to(value, step):
    return -(-value // step) * step


def dot(a, b):
    return jnp.dot(a, b, preferred_element_type=F32)


def dot_nt(a, b):
    return lax.dot_general(a, b, (((1,), (1,)), ((), ())), preferred_element_type=F32)


def layer(
    sizes,
    q_hbm,
    keys_hbm,
    values_hbm,
    fresh_hbm,
    lengths_hbm,
    residual_hbm,
    gain_hbm,
    wo_hbm,
    gate_up_hbm,
    down_hbm,
    routed_hbm,
    router_hbm,
    out_ref,
    q_ref,
    keys_ref,
    values_ref,
    fresh_ref,
    lengths_ref,
    residual_ref,
    gain_ref,
    wo_ref,
    gate_up_ref,
    down_ref,
    routed_ref,
    router_ref,
    att,
    psend,
    prec,
    mixed_ref,
    dsend,
    drecv,
    hbuf,
    rsend,
    rrecv,
    load_sem,
    att_send,
    att_recv,
    p_send,
    p_recv,
    d_send,
    d_recv,
    h_send,
    h_recv,
    r_send,
    r_recv,
):
    wide, narrow, deep = sizes
    experts = wide * deep
    my_wide = lax.axis_index("wide")
    my_narrow = lax.axis_index("narrow")
    my_deep = lax.axis_index("deep")
    my_expert = my_wide * deep + my_deep
    my_quad = my_narrow * deep + my_deep

    rows, local_heads, length, head = keys_ref.shape
    group = q_ref.shape[1] // (local_heads * head)
    width = residual_ref.shape[1]
    part = wo_ref.shape[1]
    share = down_ref.shape[2]
    units = gate_up_ref.shape[2]
    picks = routed_ref.shape[1]
    capacity = rows // 4
    slots = dsend.shape[1] // 2
    half = width // 2
    row_pad = att.shape[2]

    def device(w, n, d):
        return {"wide": w, "narrow": n, "deep": d}

    hbm = (
        q_hbm, fresh_hbm, lengths_hbm, keys_hbm, values_hbm, routed_hbm, router_hbm,
        residual_hbm, gain_hbm, wo_hbm, gate_up_hbm, down_hbm,
    )
    local = (
        q_ref, fresh_ref, lengths_ref, keys_ref, values_ref, routed_ref, router_ref,
        residual_ref, gain_ref, wo_ref, gate_up_ref, down_ref,
    )
    loads = [
        pltpu.make_async_copy(src, dst, load_sem.at[at])
        for at, (src, dst) in enumerate(zip(hbm, local))
    ]
    for load in loads:
        load.start()

    barrier = pltpu.get_barrier_semaphore()
    greeted = 0
    for off in range(1, narrow * deep):
        other = lax.rem(my_quad + off, narrow * deep)
        pl.semaphore_signal(
            barrier, inc=1, device_id=device(my_wide, other // deep, lax.rem(other, deep)),
            device_id_type=MESH,
        )
        greeted += 1
    for w_off in range(1, wide):
        other_wide = lax.rem(my_wide + w_off, wide)
        for d in range(deep):
            pl.semaphore_signal(
                barrier, inc=1, device_id=device(other_wide, my_narrow, d), device_id_type=MESH
            )
            greeted += 1

    for load in loads[:5]:
        load.wait()
    block = 8
    scale = 1.0 / math.sqrt(head)
    lanes = block * length
    lane = lax.broadcasted_iota(jnp.int32, (block, lanes), 1)
    row = lax.broadcasted_iota(jnp.int32, (block, lanes), 0)
    own_block = lane // length == row
    position = lax.rem(lane, length)
    fresh = fresh_ref[...].astype(F32)
    fresh_keys = fresh[:, 0, :]
    fresh_values = fresh[:, 1, :]
    masks = []
    for r in range(rows // block):
        limit = jnp.zeros((block, lanes), jnp.int32)
        for i in range(block):
            limit = jnp.where(row == i, lengths_ref[r * block + i], limit)
        valid = own_block & (position < limit)
        bias = jnp.where(valid, 0.0, -1e30).astype(F32)
        masks.append(jnp.concatenate([bias] * group, 0))
    copies = []
    for k in range(local_heads):
        queries = q_ref[:, k * group * head : (k + 1) * group * head].astype(F32)
        pieces = []
        for r in range(rows // block):
            at = slice(r * block, (r + 1) * block)
            query = jnp.concatenate(
                [queries[at, h * head : (h + 1) * head] for h in range(group)], 0
            )
            keys = keys_ref[at, k].reshape(lanes, head)
            values = values_ref[at, k].reshape(lanes, head)
            new_key = jnp.concatenate([fresh_keys[at, k * head : (k + 1) * head]] * group, 0)
            new_value = jnp.concatenate([fresh_values[at, k * head : (k + 1) * head]] * group, 0)
            keep = masks[r] == 0.0
            scores = jnp.where(keep, dot_nt(query.astype(BF), keys) * scale, -1e30)
            own = jnp.sum(query * new_key, -1, keepdims=True) * scale
            top = jnp.maximum(jnp.max(scores, -1, keepdims=True), own)
            raw = jnp.exp(scores - top)
            own_raw = jnp.exp(own - top)
            total = jnp.sum(raw, -1, keepdims=True) + own_raw
            probs = (raw / total).astype(BF)
            own_prob = (own_raw / total).astype(BF).astype(F32)
            result = dot(probs, values) + own_prob * new_value
            pieces.append(
                jnp.concatenate([result[h * block : (h + 1) * block] for h in range(group)], 1)
            )
        if row_pad > rows:
            pieces.append(jnp.zeros((row_pad - rows, group * head), F32))
        att[k, my_deep] = jnp.concatenate(pieces, 0).astype(BF)
        if k == 0:
            pl.semaphore_wait(barrier, greeted)
        for off in range(1, deep):
            other = lax.rem(my_deep + off, deep)
            copy = pltpu.make_async_remote_copy(
                src_ref=att.at[k, my_deep],
                dst_ref=att.at[k, my_deep],
                send_sem=att_send.at[k, other],
                recv_sem=att_recv.at[k, my_deep],
                device_id=device(my_wide, my_narrow, other),
                device_id_type=MESH,
            )
            copy.start()
            copies.append(copy)

    loads[5].wait()
    loads[6].wait()
    routed = routed_ref[...]
    router = router_ref[...]
    shares = router / jnp.sum(router, -1, keepdims=True)
    wide_slots = experts * 2 * slots
    slot_lane = lax.broadcasted_iota(jnp.int32, (rows, wide_slots), 1)
    lane_expert = slot_lane // (2 * slots)
    lane_place = lax.rem(slot_lane, 2 * slots)
    named = [lane_expert == routed[:, j : j + 1] for j in range(picks)]
    hits = jnp.zeros((rows, wide_slots), F32)
    for j in range(picks):
        hits = hits + jnp.where(named[j], 1.0, 0.0)
    earlier = (
        lax.broadcasted_iota(jnp.int32, (rows, rows), 0)
        > lax.broadcasted_iota(jnp.int32, (rows, rows), 1)
    )
    before = dot(jnp.where(earlier, 1.0, 0.0).astype(BF), hits.astype(BF))
    place = lane_place.astype(F32)
    low = before == place
    high = before + slots == place
    placing_low = jnp.where(low, hits, 0.0)
    placing_high = jnp.where(high, hits, 0.0)

    loads[9].wait()
    acc = None
    for k in range(local_heads):
        for off in range(1, deep):
            other = lax.rem(my_deep + off, deep)
            pltpu.make_async_remote_copy(
                src_ref=att.at[k, other],
                dst_ref=att.at[k, other],
                send_sem=att_send.at[k, other],
                recv_sem=att_recv.at[k, other],
                device_id=device(my_wide, my_narrow, other),
                device_id_type=MESH,
            ).wait_recv()
        term = dot(
            att[k].reshape(deep * row_pad, group * head),
            wo_ref[k * group * head : (k + 1) * group * head, :],
        )
        acc = term if acc is None else acc + term
    for d in range(deep):
        mine = acc[d * row_pad : d * row_pad + rows]
        psend[d] = jnp.concatenate([mine[:, : part // 2], mine[:, part // 2 :]], 0).astype(BF)
    for off in range(1, narrow * deep):
        other = lax.rem(my_quad + off, narrow * deep)
        other_deep = lax.rem(other, deep)
        copy = pltpu.make_async_remote_copy(
            src_ref=psend.at[other_deep],
            dst_ref=prec.at[my_quad],
            send_sem=p_send.at[other],
            recv_sem=p_recv.at[my_quad],
            device_id=device(my_wide, other // deep, other_deep),
            device_id_type=MESH,
        )
        copy.start()
        copies.append(copy)
    prec[my_quad] = psend[my_deep]

    loads[7].wait()
    loads[8].wait()
    for off in range(1, narrow * deep):
        other = lax.rem(my_quad + off, narrow * deep)
        pltpu.make_async_remote_copy(
            src_ref=psend.at[0],
            dst_ref=prec.at[other],
            send_sem=p_send.at[other],
            recv_sem=p_recv.at[other],
            device_id=device(my_wide, other // deep, lax.rem(other, deep)),
            device_id_type=MESH,
        ).wait_recv()
    projected = []
    for d in range(deep):
        total = prec[d].astype(F32)
        for n in range(1, narrow):
            total = total + prec[n * deep + d].astype(F32)
        projected += [total[:rows], total[rows:]]
    mixed = residual_ref[...].astype(F32) + jnp.concatenate(projected, 1)
    mixed_ref[...] = mixed
    squares = jnp.sum(mixed * mixed, -1, keepdims=True)
    normed = (mixed * lax.rsqrt(squares / width + 1e-06) * gain_ref[...]).astype(BF)
    outgoing_low = lax.dot_general(
        placing_low.T.astype(BF), normed[:, :half], (((1,), (0,)), ((), ())),
        preferred_element_type=F32,
    )
    outgoing_high = lax.dot_general(
        placing_high.T.astype(BF), normed[:, half:], (((1,), (0,)), ((), ())),
        preferred_element_type=F32,
    )
    dsend[...] = (outgoing_low + outgoing_high).astype(BF).reshape(experts, 2 * slots, half)
    for off in range(1, experts):
        other = lax.rem(my_expert + off, experts)
        copy = pltpu.make_async_remote_copy(
            src_ref=dsend.at[other],
            dst_ref=drecv.at[my_expert],
            send_sem=d_send.at[other],
            recv_sem=d_recv.at[my_expert],
            device_id=device(other // deep, my_narrow, lax.rem(other, deep)),
            device_id_type=MESH,
        )
        copy.start()
        copies.append(copy)
    drecv[my_expert] = dsend[my_expert]

    loads[10].wait()
    for off in range(1, experts):
        other = lax.rem(my_expert + off, experts)
        pltpu.make_async_remote_copy(
            src_ref=dsend.at[other],
            dst_ref=drecv.at[other],
            send_sem=d_send.at[other],
            recv_sem=d_recv.at[other],
            device_id=device(other // deep, my_narrow, lax.rem(other, deep)),
            device_id_type=MESH,
        ).wait_recv()
    arrived = drecv[...].reshape(experts * 2 * slots, half)
    both = []
    for g in range(2):
        low_part = dot_nt(arrived, gate_up_ref[0, g, :, :half])
        high_part = dot_nt(arrived, gate_up_ref[0, g, :, half:])
        low_part = low_part.reshape(experts, 2 * slots, units)[:, :slots]
        high_part = high_part.reshape(experts, 2 * slots, units)[:, slots:]
        both.append((low_part + high_part).reshape(experts * slots, units))
    hidden = (both[0] / (1.0 + jnp.exp(-both[0])) * both[1]).astype(BF)
    hbuf[my_narrow] = hidden
    for off in range(1, narrow):
        other = lax.rem(my_narrow + off, narrow)
        copy = pltpu.make_async_remote_copy(
            src_ref=hbuf.at[my_narrow],
            dst_ref=hbuf.at[my_narrow],
            send_sem=h_send.at[other],
            recv_sem=h_recv.at[my_narrow],
            device_id=device(my_wide, other, my_deep),
            device_id_type=MESH,
        )
        copy.start()
        copies.append(copy)

    loads[11].wait()

    def down_rows(n):
        return down_ref[0, pl.ds(pl.multiple_of(n * units, units), units), :]

    result = dot(hidden, down_rows(my_narrow))
    for off in range(1, narrow):
        other = lax.rem(my_narrow + off, narrow)
        pltpu.make_async_remote_copy(
            src_ref=hbuf.at[other],
            dst_ref=hbuf.at[other],
            send_sem=h_send.at[other],
            recv_sem=h_recv.at[other],
            device_id=device(my_wide, other, my_deep),
            device_id_type=MESH,
        ).wait_recv()
        result = result + dot(hbuf[other], down_rows(other))
    result = result.reshape(experts, slots, share)
    rsend[...] = jnp.concatenate(
        [result[:, :, : share // 2], result[:, :, share // 2 :]], 1
    ).astype(BF)
    for off in range(1, experts):
        other = lax.rem(my_expert + off, experts)
        copy = pltpu.make_async_remote_copy(
            src_ref=rsend.at[other],
            dst_ref=rrecv.at[my_expert],
            send_sem=r_send.at[other],
            recv_sem=r_recv.at[my_expert],
            device_id=device(other // deep, my_narrow, lax.rem(other, deep)),
            device_id_type=MESH,
        )
        copy.start()
        copies.append(copy)
    rrecv[my_expert] = rsend[my_expert]

    for off in range(1, experts):
        other = lax.rem(my_expert + off, experts)
        pltpu.make_async_remote_copy(
            src_ref=rsend.at[other],
            dst_ref=rrecv.at[other],
            send_sem=r_send.at[other],
            recv_sem=r_recv.at[other],
            device_id=device(other // deep, my_narrow, lax.rem(other, deep)),
            device_id_type=MESH,
        ).wait_recv()
    returned = rrecv[...].reshape(experts * 2 * slots, share // 2)
    sums = []
    for side in (low, high):
        combined = None
        for j in range(picks):
            pick = jnp.where(named[j] & side, 1.0, 0.0).astype(BF)
            term = dot(pick, returned) * shares[:, j : j + 1]
            combined = term if combined is None else combined + term
        sums.append(combined)
    my_columns = pl.ds(pl.multiple_of(my_narrow * share, share), share)
    out_ref[...] = (mixed_ref[:, my_columns] + jnp.concatenate(sums, 1)).astype(BF)
    for copy in copies:
        copy.wait_send()


def shards(sizes, *operands):
    (queries, cache_keys, cache_values, fresh_pairs, lengths, residual, norm_gain,
     output_weight, expert_gate_up, expert_down, routed_experts, router_weights) = operands
    wide, narrow, deep = sizes
    experts = wide * deep
    rows = queries.shape[0]
    local_heads = cache_keys.shape[1]
    width = residual.shape[1]
    part = output_weight.shape[1]
    units = expert_gate_up.shape[2]
    share = expert_down.shape[2]
    slots = up_to(rows // 4, 8)
    operands = (queries, cache_keys, cache_values, fresh_pairs, lengths, residual,
                norm_gain.reshape(1, width), output_weight, expert_gate_up, expert_down,
                routed_experts, router_weights)
    dma = pltpu.SemaphoreType.DMA
    held = [
        pltpu.SMEM(x.shape, x.dtype) if x is lengths else pltpu.VMEM(x.shape, x.dtype)
        for x in operands
    ]
    return pl.pallas_call(
        functools.partial(layer, sizes),
        out_shape=jax.ShapeDtypeStruct((rows, share), BF),
        in_specs=[pl.BlockSpec(memory_space=pl.ANY)] * len(operands),
        out_specs=pl.BlockSpec(memory_space=pltpu.VMEM),
        scratch_shapes=held
        + [
            pltpu.VMEM((local_heads, deep, up_to(rows, 16), queries.shape[1] // local_heads), BF),
            pltpu.VMEM((deep, 2 * rows, part // 2), BF),
            pltpu.VMEM((narrow * deep, 2 * rows, part // 2), BF),
            pltpu.VMEM((rows, width), F32),
            pltpu.VMEM((experts, 2 * slots, width // 2), BF),
            pltpu.VMEM((experts, 2 * slots, width // 2), BF),
            pltpu.VMEM((narrow, experts * slots, units), BF),
            pltpu.VMEM((experts, 2 * slots, share // 2), BF),
            pltpu.VMEM((experts, 2 * slots, share // 2), BF),
            dma((len(operands),)),
            dma((local_heads, deep)),
            dma((local_heads, deep)),
            dma((narrow * deep,)),
            dma((narrow * deep,)),
            dma((experts,)),
            dma((experts,)),
            dma((narrow,)),
            dma((narrow,)),
            dma((experts,)),
            dma((experts,)),
        ],
        compiler_params=pltpu.CompilerParams(
            collective_id=0, has_side_effects=True, vmem_limit_bytes=48 * 1024 * 1024
        ),
    )(*operands)


def solution(mesh):
    in_specs = (
        P(("group", "wide", "deep"), "narrow"),
        P(("group", "wide", "deep"), "narrow", None, None),
        P(("group", "wide", "deep"), "narrow", None, None),
        P(("group", "wide", "deep"), None, "narrow"),
        P(("group", "wide", "deep")),
        P(("group", "wide", "deep"), None),
        P(),
        P("narrow", "deep"),
        P(("wide", "deep"), None, "narrow", None),
        P(("wide", "deep"), None, "narrow"),
        P(("group", "wide", "deep"), None),
        P(("group", "wide", "deep"), None),
    )
    out_specs = P(("group", "wide", "deep"), "narrow")
    sizes = (mesh.shape["wide"], mesh.shape["narrow"], mesh.shape["deep"])
    return jax.shard_map(
        functools.partial(shards, sizes), mesh=mesh, in_specs=in_specs, out_specs=out_specs,
        check_vma=False,
    )
```

time: 82.8 us -> 41.2 us (0.50)
  Pallas kernels: 0 us -> 29.5 us
  waiting for transfers between devices: 25.8 us -> 0 us
  blocking collectives: 20.8 us -> 0 us
  between operations: 13.6 us -> 0.02 us
  starting transfers between devices: 7.98 us -> 0 us
  local copies, waits for them, and re-layouts: 4.57 us -> 11.2 us
  matrix products: 6.37 us -> 0 us
  other arithmetic: 3.07 us -> 0 us
    pallas_call x0 -> x1, Pallas kernels: none -> 29.5 us  [shards(): pl.pallas_call(functools.partial(layer, sizes), out_shape=jax.ShapeDtypeS...]
    all_to_all x2 -> x0, waiting for transfers between devices: 13.4 us -> none  [the longest x1 6.76 us: shards(): lax.all_to_all(outgoing, ('wide', 'deep'), split_axis=0, concat_axis=0, t...]
    reduce_scatter x1 -> x0, waiting for transfers between devices: 12.4 us -> none  [shards(): lax.psum_scatter(partial_value.astype(jnp.bfloat16), 'narrow', scatter_di...]
    all_gather x3 -> x0, blocking collectives: 12.1 us -> none  [the longest x1 5.43 us: shards(): lax.all_gather(incoming, 'narrow', axis=1, tiled=True)]
    unnamed x18 -> x21, local copies, waits for them, and re-layouts: 1.13 us -> 11.2 us
    all_to_all x2 -> x0, starting transfers between devices: 7.98 us -> none  [the longest x1 4.61 us: shards(): lax.all_to_all(outgoing, ('wide', 'deep'), split_axis=0, concat_axis=0, t...]
    dot_general x7 -> x0, matrix products: 6.37 us -> none  [the longest x1 1.57 us: shards(): jnp.einsum('rkgd,rkld->rkgl', query_heads, cache_keys, preferred_element_...]
    psum x1 -> x0, blocking collectives: 4.94 us -> none  [shards(): lax.psum(jnp.sum(mixed_mine * mixed_mine, -1, keepdims=True), 'narrow')]
  transfers between devices with their start and end apart: 3 -> 0, of which waited for: 3 -> 0; matrix products, arithmetic and copies ran while one was open for 0% -> 0% of each run, Pallas kernels for 0% -> 0%
where the time goes in v1:
time: 41.2 us; the launch traced here: 40.8 us
  Pallas kernels  29.5 us (72%)
  local copies, waits for them, and re-layouts  11.2 us (27%)
    pallas_call x1, Pallas kernels, shards(): pl.pallas_call(functools.partial(layer, sizes), out_shape=jax.ShapeDtypeS...  29.5 us
    unnamed x21, local copies, waits for them, and re-layouts  11.2 us

profile of v1, /device:TPU:0, one launch (start us, length us, event | category | flops | bytes accessed | tf_op | source)
XLA Modules:
  0.0 40.8 jit_solution(9509251878975042684)
XLA Ops:
  0.0 0.7 %copy.13.routed_hbm = s32[24,1]{1,0:T(8,128)S(1)} copy(s32[24,1]{0,1:T(1,128)} %param.22) | data formatting | bytes 192 | tf_op args[10]
  0.7 0.7 %copy.14.router_hbm = f32[24,1]{1,0:T(8,128)S(1)} copy(f32[24,1]{0,1:T(1,128)} %param.23) | data formatting | bytes 192 | tf_op args[11]
  1.5 0.0 copy-start
  1.5 1.9 %copy-done = bf16[1,2,384,2048]{3,2,1,0:T(8,128)(2,1)S(1)} copy-done((bf16[1,2,384,2048]{3,2,1,0:T(8,128)(2,1)S(1)}, bf16[1,2,384,2048]{3,2,1,0:T(8,128)(2,1)}, u32[]{:S(2)}) %copy-start) | copy-done | bytes 3145752
  3.4 0.0 copy-start.1
  3.4 1.4 %copy-done.1 = bf16[1,768,1024]{2,1,0:T(8,128)(2,1)S(1)} copy-done((bf16[1,768,1024]{2,1,0:T(8,128)(2,1)S(1)}, bf16[1,768,1024]{2,1,0:T(8,128)(2,1)}, u32[]{:S(2)}) %copy-start.1) | copy-done | bytes 1572888
  4.8 0.0 copy-start.2
  4.8 1.0 %copy-done.2 = bf16[24,2,32,128]{3,2,1,0:T(8,128)(2,1)S(1)} copy-done((bf16[24,2,32,128]{3,2,1,0:T(8,128)(2,1)S(1)}, bf16[24,2,32,128]{3,2,1,0:T(8,128)(2,1)}, u32[]{:S(2)}) %copy-start.2) | copy-done | bytes 393240
  5.8 0.0 copy-start.3
  5.8 1.0 %copy-done.3 = bf16[24,2,32,128]{3,2,1,0:T(8,128)(2,1)S(1)} copy-done((bf16[24,2,32,128]{3,2,1,0:T(8,128)(2,1)S(1)}, bf16[24,2,32,128]{3,2,1,0:T(8,128)(2,1)}, u32[]{:S(2)}) %copy-start.3) | copy-done | bytes 393240
  6.8 0.0 copy-start.4
  6.8 0.9 %copy-done.4 = bf16[24,2048]{1,0:T(8,128)(2,1)S(1)} copy-done((bf16[24,2048]{1,0:T(8,128)(2,1)S(1)}, bf16[24,2048]{1,0:T(8,128)(2,1)}, u32[]{:S(2)}) %copy-start.4) | copy-done | bytes 98328
  7.7 0.0 copy-start.5
  7.7 0.9 %copy-done.5 = bf16[24,2048]{1,0:T(8,128)(2,1)S(1)} copy-done((bf16[24,2048]{1,0:T(8,128)(2,1)S(1)}, bf16[24,2048]{1,0:T(8,128)(2,1)}, u32[]{:S(2)}) %copy-start.5) | copy-done | bytes 98328
  8.5 0.0 copy-start.6
  8.5 0.7 %copy-done.6 = bf16[24,2,256]{2,1,0:T(2,128)(2,1)S(1)} copy-done((bf16[24,2,256]{2,1,0:T(2,128)(2,1)S(1)}, bf16[24,2,256]{2,1,0:T(2,128)(2,1)}, u32[]{:S(2)}) %copy-start.6) | copy-done | bytes 24600
  9.3 0.0 copy-start.7
  9.3 0.7 %copy-done.7 = f32[2048]{0:T(1024)S(1)} copy-done((f32[2048]{0:T(1024)S(1)}, f32[2048]{0:T(1024)}, u32[]{:S(2)}) %copy-start.7) | copy-done | bytes 8216
  10.0 0.0 copy-start.8
  10.0 0.7 %copy-done.8 = s32[24]{0:T(128)S(1)} copy-done((s32[24]{0:T(128)S(1)}, s32[24]{0:T(128)}, u32[]{:S(2)}) %copy-start.8) | copy-done | bytes 120
  10.6 29.5 %shard_map.118 = bf16[24,1024]{1,0:T(8,128)(2,1)S(1)} custom-call(bf16[24,2048]{1,0:T(8,128)(2,1)S(1)} %copy-done.4, bf16[24,2,32,128]{3,2,1,0:T(8,128)(2,1)S(1)} %copy-done.2, bf16[24,2,32,128]{3,2,1,0:T(8,128)(2,1)S(1)} %copy-done.3, bf16[24,2,256]{2,1,0:T(2,128)(2,1)S(1)} %copy-done.6, s32[24]{0:T(128)S(1)} %copy-done.8, bf16[24,2048]{1,0:T(8,128)(2,1)S(1)} %copy-done.5, ...), custom_call_target="tpu_custom_call" | custom-call | tf_op jit(solution)/shard_map/pallas_call | solution.py:414
  40.1 0.6 %copy.16 = bf16[24,1024]{1,0:T(8,128)(2,1)} copy(bf16[24,1024]{1,0:T(8,128)(2,1)S(1)} %shard_map.118) | data formatting | bytes 98304
Async XLA Ops:
  1.5 1.9 %copy-start = (bf16[1,2,384,2048]{3,2,1,0:T(8,128)(2,1)S(1)}, bf16[1,2,384,2048]{3,2,1,0:T(8,128)(2,1)}, u32[]{:S(2)}) copy-start(bf16[1,2,384,2048]{3,2,1,0:T(8,128)(2,1)} %gate_up_hbm.1) | copy-start | bytes 9437188
  3.4 1.4 %copy-start.1 = (bf16[1,768,1024]{2,1,0:T(8,128)(2,1)S(1)}, bf16[1,768,1024]{2,1,0:T(8,128)(2,1)}, u32[]{:S(2)}) copy-start(bf16[1,768,1024]{2,1,0:T(8,128)(2,1)} %down_hbm.1) | copy-start | bytes 4718596
  4.8 1.0 %copy-start.2 = (bf16[24,2,32,128]{3,2,1,0:T(8,128)(2,1)S(1)}, bf16[24,2,32,128]{3,2,1,0:T(8,128)(2,1)}, u32[]{:S(2)}) copy-start(bf16[24,2,32,128]{3,2,1,0:T(8,128)(2,1)} %keys_hbm.1) | copy-start | bytes 1179652
  5.8 1.0 %copy-start.3 = (bf16[24,2,32,128]{3,2,1,0:T(8,128)(2,1)S(1)}, bf16[24,2,32,128]{3,2,1,0:T(8,128)(2,1)}, u32[]{:S(2)}) copy-start(bf16[24,2,32,128]{3,2,1,0:T(8,128)(2,1)} %values_hbm.1) | copy-start | bytes 1179652
  6.8 0.9 %copy-start.4 = (bf16[24,2048]{1,0:T(8,128)(2,1)S(1)}, bf16[24,2048]{1,0:T(8,128)(2,1)}, u32[]{:S(2)}) copy-start(bf16[24,2048]{1,0:T(8,128)(2,1)} %q_hbm.1) | copy-start | bytes 294916
  7.7 0.9 %copy-start.5 = (bf16[24,2048]{1,0:T(8,128)(2,1)S(1)}, bf16[24,2048]{1,0:T(8,128)(2,1)}, u32[]{:S(2)}) copy-start(bf16[24,2048]{1,0:T(8,128)(2,1)} %residual_hbm.1) | copy-start | bytes 294916
  8.5 0.7 %copy-start.6 = (bf16[24,2,256]{2,1,0:T(2,128)(2,1)S(1)}, bf16[24,2,256]{2,1,0:T(2,128)(2,1)}, u32[]{:S(2)}) copy-start(bf16[24,2,256]{2,1,0:T(2,128)(2,1)} %fresh_hbm.1) | copy-start | bytes 73732
  9.3 0.7 %copy-start.7 = (f32[2048]{0:T(1024)S(1)}, f32[2048]{0:T(1024)}, u32[]{:S(2)}) copy-start(f32[2048]{0:T(1024)} %param.18) | copy-start | bytes 24580
  10.0 0.7 %copy-start.8 = (s32[24]{0:T(128)S(1)}, s32[24]{0:T(128)}, u32[]{:S(2)}) copy-start(s32[24]{0:T(128)} %lengths_hbm.1) | copy-start | bytes 292

commit v2 on v1

--- a/solution.py
+++ b/solution.py
@@ -87,7 +87,7 @@
     part = wo_ref.shape[1]
     share = down_ref.shape[2]
     units = gate_up_ref.shape[2]
-    picks = routed_ref.shape[1]
+    picks = routed_ref.shape[0]
     capacity = rows // 4
     slots = dsend.shape[1] // 2
     half = width // 2
@@ -194,22 +194,27 @@
 
     loads[5].wait()
     loads[6].wait()
-    routed = routed_ref[...]
+    square = (rows, rows)
+    down_at = lax.broadcasted_iota(jnp.int32, square, 0)
+    across_at = lax.broadcasted_iota(jnp.int32, square, 1)
+
+    def column(line):
+        spread = jnp.where(down_at == across_at, line, jnp.zeros_like(line))
+        return jnp.sum(spread, -1, keepdims=True)
+
     router = router_ref[...]
-    shares = router / jnp.sum(router, -1, keepdims=True)
+    shares = router / jnp.sum(router, 0, keepdims=True)
+    shares = [column(shares[j : j + 1, :]) for j in range(picks)]
+    routed = [column(routed_ref[j : j + 1, :]) for j in range(picks)]
     wide_slots = experts * 2 * slots
     slot_lane = lax.broadcasted_iota(jnp.int32, (rows, wide_slots), 1)
     lane_expert = slot_lane // (2 * slots)
     lane_place = lax.rem(slot_lane, 2 * slots)
-    named = [lane_expert == routed[:, j : j + 1] for j in range(picks)]
+    named = [lane_expert == routed[j] for j in range(picks)]
     hits = jnp.zeros((rows, wide_slots), F32)
     for j in range(picks):
         hits = hits + jnp.where(named[j], 1.0, 0.0)
-    earlier = (
-        lax.broadcasted_iota(jnp.int32, (rows, rows), 0)
-        > lax.broadcasted_iota(jnp.int32, (rows, rows), 1)
-    )
-    before = dot(jnp.where(earlier, 1.0, 0.0).astype(BF), hits.astype(BF))
+    before = dot(jnp.where(down_at > across_at, 1.0, 0.0).astype(BF), hits.astype(BF))
     place = lane_place.astype(F32)
     low = before == place
     high = before + slots == place
@@ -382,7 +387,7 @@
         combined = None
         for j in range(picks):
             pick = jnp.where(named[j] & side, 1.0, 0.0).astype(BF)
-            term = dot(pick, returned) * shares[:, j : j + 1]
+            term = dot(pick, returned) * shares[j]
             combined = term if combined is None else combined + term
         sums.append(combined)
     my_columns = pl.ds(pl.multiple_of(my_narrow * share, share), share)
@@ -405,7 +410,7 @@
     slots = up_to(rows // 4, 8)
     operands = (queries, cache_keys, cache_values, fresh_pairs, lengths, residual,
                 norm_gain.reshape(1, width), output_weight, expert_gate_up, expert_down,
-                routed_experts, router_weights)
+                routed_experts.T, router_weights.T)
     dma = pltpu.SemaphoreType.DMA
     held = [
         pltpu.SMEM(x.shape, x.dtype) if x is lengths else pltpu.VMEM(x.shape, x.dtype)
@@ -440,7 +445,7 @@
             dma((experts,)),
         ],
         compiler_params=pltpu.CompilerParams(
-            collective_id=0, has_side_effects=True, vmem_limit_bytes=48 * 1024 * 1024
+            collective_id=0, has_side_effects=True, vmem_limit_bytes=63 * 1024 * 1024
         ),
     )(*operands)
 

time: 41.2 us -> 30.7 us (0.75)
  local copies, waits for them, and re-layouts: 11.2 us -> 1.42 us
    unnamed x21 -> x1, local copies, waits for them, and re-layouts: 11.2 us -> 1.42 us
where the time goes in v2:
time: 30.7 us; the launch traced here: 30.6 us
  Pallas kernels  29.1 us (95%)
  local copies, waits for them, and re-layouts  1.42 us (5%)
    pallas_call x1, Pallas kernels, shards(): pl.pallas_call(functools.partial(layer, sizes), out_shape=jax.ShapeDtypeS...  29.1 us
    unnamed x1, local copies, waits for them, and re-layouts  1.42 us

profile of v2, /device:TPU:0, one launch (start us, length us, event | category | flops | bytes accessed | tf_op | source)
XLA Modules:
  0.0 30.6 jit_solution(13048494256753156143)
XLA Ops:
  0.0 29.1 %shard_map.118 = bf16[24,1024]{1,0:T(8,128)(2,1)} custom-call(bf16[24,2048]{1,0:T(8,128)(2,1)} %q_hbm.1, bf16[24,2,32,128]{3,2,1,0:T(8,128)(2,1)} %keys_hbm.1, bf16[24,2,32,128]{3,2,1,0:T(8,128)(2,1)} %values_hbm.1, bf16[24,2,256]{2,1,0:T(2,128)(2,1)} %fresh_hbm.1, s32[24]{0:T(128)} %lengths_hbm.1, bf16[24,2048]{1,0:T(8,128)(2,1)} %residual_hbm.1, ...), custom_call_target="tpu_custom_call" | custom-call | tf_op jit(solution)/shard_map/pallas_call | solution.py:419
  29.1 1.4 %copy.14 = bf16[24,1024]{1,0:T(8,128)(2,1)} copy(bf16[24,1024]{1,0:T(8,128)(2,1)} %shard_map.118) | data formatting | bytes 98304

commit v3 on v2

--- a/solution.py
+++ b/solution.py
@@ -96,6 +96,8 @@
     def device(w, n, d):
         return {"wide": w, "narrow": n, "deep": d}
 
+    far_first = sorted(range(1, experts), key=lambda off: abs(2 * off - experts))
+
     hbm = (
         q_hbm, fresh_hbm, lengths_hbm, keys_hbm, values_hbm, routed_hbm, router_hbm,
         residual_hbm, gain_hbm, wo_hbm, gate_up_hbm, down_hbm,
@@ -148,7 +150,6 @@
         valid = own_block & (position < limit)
         bias = jnp.where(valid, 0.0, -1e30).astype(F32)
         masks.append(jnp.concatenate([bias] * group, 0))
-    copies = []
     for k in range(local_heads):
         queries = q_ref[:, k * group * head : (k + 1) * group * head].astype(F32)
         pieces = []
@@ -177,20 +178,6 @@
         if row_pad > rows:
             pieces.append(jnp.zeros((row_pad - rows, group * head), F32))
         att[k, my_deep] = jnp.concatenate(pieces, 0).astype(BF)
-        if k == 0:
-            pl.semaphore_wait(barrier, greeted)
-        for off in range(1, deep):
-            other = lax.rem(my_deep + off, deep)
-            copy = pltpu.make_async_remote_copy(
-                src_ref=att.at[k, my_deep],
-                dst_ref=att.at[k, my_deep],
-                send_sem=att_send.at[k, other],
-                recv_sem=att_recv.at[k, my_deep],
-                device_id=device(my_wide, my_narrow, other),
-                device_id_type=MESH,
-            )
-            copy.start()
-            copies.append(copy)
 
     loads[5].wait()
     loads[6].wait()
@@ -221,6 +208,22 @@
     placing_low = jnp.where(low, hits, 0.0)
     placing_high = jnp.where(high, hits, 0.0)
 
+    pl.semaphore_wait(barrier, greeted)
+    copies = []
+    for k in range(local_heads):
+        for off in range(1, deep):
+            other = lax.rem(my_deep + off, deep)
+            copy = pltpu.make_async_remote_copy(
+                src_ref=att.at[k, my_deep],
+                dst_ref=att.at[k, my_deep],
+                send_sem=att_send.at[k, other],
+                recv_sem=att_recv.at[k, my_deep],
+                device_id=device(my_wide, my_narrow, other),
+                device_id_type=MESH,
+            )
+            copy.start()
+            copies.append(copy)
+
     loads[9].wait()
     acc = None
     for k in range(local_heads):
@@ -288,7 +291,7 @@
         preferred_element_type=F32,
     )
     dsend[...] = (outgoing_low + outgoing_high).astype(BF).reshape(experts, 2 * slots, half)
-    for off in range(1, experts):
+    for off in far_first:
         other = lax.rem(my_expert + off, experts)
         copy = pltpu.make_async_remote_copy(
             src_ref=dsend.at[other],
@@ -303,7 +306,7 @@
     drecv[my_expert] = dsend[my_expert]
 
     loads[10].wait()
-    for off in range(1, experts):
+    for off in far_first:
         other = lax.rem(my_expert + off, experts)
         pltpu.make_async_remote_copy(
             src_ref=dsend.at[other],
@@ -357,7 +360,7 @@
     rsend[...] = jnp.concatenate(
         [result[:, :, : share // 2], result[:, :, share // 2 :]], 1
     ).astype(BF)
-    for off in range(1, experts):
+    for off in far_first:
         other = lax.rem(my_expert + off, experts)
         copy = pltpu.make_async_remote_copy(
             src_ref=rsend.at[other],
@@ -371,7 +374,7 @@
         copies.append(copy)
     rrecv[my_expert] = rsend[my_expert]
 
-    for off in range(1, experts):
+    for off in far_first:
         other = lax.rem(my_expert + off, experts)
         pltpu.make_async_remote_copy(
             src_ref=rsend.at[other],
@@ -418,7 +421,7 @@
     ]
     return pl.pallas_call(
         functools.partial(layer, sizes),
-        out_shape=jax.ShapeDtypeStruct((rows, share), BF),
+        out_shape=pltpu.VMEM((rows, share), BF),
         in_specs=[pl.BlockSpec(memory_space=pl.ANY)] * len(operands),
         out_specs=pl.BlockSpec(memory_space=pltpu.VMEM),
         scratch_shapes=held

time: 30.7 us -> 29.1 us (0.948)
  local copies, waits for them, and re-layouts: 1.42 us -> 0.62 us
  Pallas kernels: 29.1 us -> 28.4 us
    unnamed x1, local copies, waits for them, and re-layouts: 1.42 us -> 0.62 us
    pallas_call x1, Pallas kernels: 29.1 us -> 28.4 us  [shards(): pl.pallas_call(functools.partial(layer, sizes), out_shape=pltpu.VMEM((row...]
where the time goes in v3:
time: 29.1 us; the launch traced here: 29 us
  Pallas kernels  28.4 us (98%)
  local copies, waits for them, and re-layouts  0.62 us (2%)
    pallas_call x1, Pallas kernels, shards(): pl.pallas_call(functools.partial(layer, sizes), out_shape=pltpu.VMEM((row...  28.4 us
    unnamed x1, local copies, waits for them, and re-layouts  0.62 us

profile of v3, /device:TPU:0, one launch (start us, length us, event | category | flops | bytes accessed | tf_op | source)
XLA Modules:
  0.0 29.0 jit_solution(8736611380314022221)
XLA Ops:
  0.0 28.4 %shard_map.118 = bf16[24,1024]{1,0:T(8,128)(2,1)S(1)} custom-call(bf16[24,2048]{1,0:T(8,128)(2,1)} %q_hbm.1, bf16[24,2,32,128]{3,2,1,0:T(8,128)(2,1)} %keys_hbm.1, bf16[24,2,32,128]{3,2,1,0:T(8,128)(2,1)} %values_hbm.1, bf16[24,2,256]{2,1,0:T(2,128)(2,1)} %fresh_hbm.1, s32[24]{0:T(128)} %lengths_hbm.1, bf16[24,2048]{1,0:T(8,128)(2,1)} %residual_hbm.1, ...), custom_call_target="tpu_custom_call" | custom-call | tf_op jit(solution)/shard_map/pallas_call | solution.py:422
  28.4 0.6 %copy.14 = bf16[24,1024]{1,0:T(8,128)(2,1)} copy(bf16[24,1024]{1,0:T(8,128)(2,1)S(1)} %shard_map.118) | data formatting | bytes 98304
